TPU v7x, 32 devices: a whole 2x2x4 slice. The times are simulated.
32 devices in a mesh: row: 4 (over y, core), col: 8 (over z, x).
Axes of the slice: x: 2, y: 2, z: 4, core: 2. Of those that a mesh axis runs over, the one named last changes fastest.
Arguments:
- tokens: bfloat16 [256, 6144], P('col', 'row'), may hold values from -6 to 6
- target: bfloat16 [256, 6144], P('col', 'row'), may hold values from -6 to 6
- w_in: bfloat16 [6144, 24576], P('row', 'col'), may hold values from -0.078125 to 0.078125
- w_out: bfloat16 [6144, 24576], P('row', 'col'), may hold values from -0.0390625 to 0.0390625
- gains: float32 [2], replicated, may hold values from 2 to 6
- u_start: float32 [2, 6144], P(None, 'row'), may hold values from -6 to 6
Outputs:
- grad_tokens: bfloat16 [256, 6144], P('col', 'row')
- grad_in: bfloat16 [6144, 24576], P('row', 'col')
- grad_out: bfloat16 [6144, 24576], P('row', 'col')
- u_next: float32 [2, 6144], P(None, 'row')
All inputs are finite; a program needn't handle non-finite values.
Results may differ from a plain program's by a relative error of at most 0.006.
Values may be sent and summed in bfloat16 or wider, within the bound.
A program may use at most 256 MiB of HBM per device.

v0:
```python
import jax
import jax.numpy as jnp
from jax import lax
from jax.sharding import PartitionSpec as P

POWER = 2


EPSILON = 1e-06
ROOT_HALF = 0.7071067811865476
INV_ROOT_TWO_PI = 0.3989422804014327


def gelu_parts(values):
    normal_cdf = 0.5 * (1.0 + jax.scipy.special.erf(values * ROOT_HALF))
    active = values * normal_cdf
    slopes = normal_cdf + values * jnp.exp(-0.5 * values * values) * INV_ROOT_TWO_PI
    return (active, slopes)


def times_left(current, weights):
    return jnp.einsum("kd,kdf->kf", current, weights, precision=lax.Precision.HIGHEST)


def times_right(weights, vectors):
    return jnp.einsum("kdf,kf->kd", weights, vectors, precision=lax.Precision.HIGHEST)


def shards(tokens, target, w_in, w_out, gains, u_start):
    weights = jnp.stack([w_in, w_out]).astype(jnp.float32)
    carried = u_start
    for iteration in range(POWER):
        right_vec = lax.psum(times_left(carried, weights), "row")
        carried, right_sq = lax.psum(
            (times_right(weights, right_vec), jnp.sum(right_vec * right_vec, axis=1)), "col"
        )
    carried_sq = lax.psum(jnp.sum(carried * carried, axis=1), "row")
    right_norm = jnp.sqrt(right_sq + EPSILON)
    right_units = right_vec / right_norm[:, None]
    sigmas = jnp.sqrt(carried_sq / (right_norm * right_norm) + EPSILON)
    left_units = carried / (right_norm * sigmas)[:, None]
    scales = gains / sigmas
    token_all = lax.all_gather(tokens, "col", axis=0, tiled=True)
    total_rows = token_all.shape[0]
    partial_hidden = jnp.dot(token_all, w_in, preferred_element_type=jnp.float32)
    hidden = scales[0] * lax.psum(partial_hidden, "row")
    active, slopes = gelu_parts(hidden)
    active_all = active.astype(jnp.bfloat16)
    block_rows = active_all
    output = scales[1] * lax.psum_scatter(
        lax.dot_general(
            block_rows, w_out, (((1,), (1,)), ((), ())), preferred_element_type=jnp.float32
        ),
        "col",
        scatter_dimension=0,
        tiled=True,
    )
    loss_scale = 1.0 / jnp.sqrt(jnp.float32(total_rows))
    grad_output = ((output - target.astype(jnp.float32)) * loss_scale).astype(jnp.bfloat16)
    grad_all = lax.all_gather(grad_output, "col", axis=0, tiled=True)
    partial_delta = jnp.dot(grad_all, w_out, preferred_element_type=jnp.float32)
    delta = scales[1] * lax.psum(partial_delta, "row")
    hidden_grad = (delta * slopes).astype(jnp.bfloat16)
    block_in = lax.dot_general(
        token_all, hidden_grad, (((0,), (0,)), ((), ())), preferred_element_type=jnp.float32
    )
    block_out = lax.dot_general(
        grad_all, active_all, (((0,), (0,)), ((), ())), preferred_element_type=jnp.float32
    )
    local_traces = jnp.stack([jnp.sum(block_in * weights[0]), jnp.sum(block_out * weights[1])])
    traces = lax.psum(local_traces, ("row", "col"))
    correct = scales * traces / sigmas
    grad_in = scales[0] * block_in - correct[0] * (left_units[0][:, None] * right_units[0][None, :])
    grad_out = scales[1] * block_out - correct[1] * (
        left_units[1][:, None] * right_units[1][None, :]
    )
    block_rows = hidden_grad
    grad_tokens = scales[0] * lax.psum_scatter(
        lax.dot_general(
            block_rows, w_in, (((1,), (1,)), ((), ())), preferred_element_type=jnp.float32
        ),
        "col",
        scatter_dimension=0,
        tiled=True,
    )
    return (
        grad_tokens.astype(jnp.bfloat16),
        grad_in.astype(jnp.bfloat16),
        grad_out.astype(jnp.bfloat16),
        left_units,
    )


def solution(mesh):
    placed = (
        P("col", "row"),
        P("col", "row"),
        P("row", "col"),
        P("row", "col"),
        P(),
        P(None, "row"),
    )
    return jax.shard_map(
        shards,
        mesh=mesh,
        in_specs=placed,
        out_specs=(P("col", "row"), P("row", "col"), P("row", "col"), P(None, "row")),
        check_vma=False,
    )
```

profile of v0, /device:TPU:0, one launch (start us, length us, event | category | flops | bytes accessed | tf_op | source)
XLA Modules:
  0.0 546.1 jit_solution(1733174632013436368)
XLA Ops:
  7.2 0.0 copy-start
  7.2 0.0 all-reduce.4.cloned.1.call-start
  7.2 34.0 %all_gather.6 = bf16[256,1536]{1,0:T(8,128)(2,1)S(1)} all-gather(bf16[32,1536]{1,0:T(8,128)(2,1)} %param.6), channel_id=1, replica_groups=mesh['row'=4,'col'=8] {'col'}, dimensions={0}, use_global_device_ids=true | all-gather | bytes 884736 | tf_op jit(solution)/shard_map/all_gather | solution.py:43
  41.3 0.0 copy-start.4
  41.3 0.9 copy-done.4
  42.2 8.1 %fusion.27 = f32[256,3072]{1,0:T(8,128)} fusion(bf16[256,1536]{1,0:T(8,128)(2,1)S(1)} %all_gather.6, bf16[1536,3072]{1,0:T(8,128)(2,1)} %param.8), kind=kOutput, calls=%fused_computation.52 | convolution fusion | flops 2415919104 | bytes 13369344 | tf_op jit(solution)/shard_map/dot_general | solution.py:45
  50.3 0.0 all-reduce.4.cloned.1.call-update
  50.3 0.0 reduce-scatter.3.cloned.1.call-start
  50.4 12.7 %copy.14 = bf16[1536,3072]{0,1:T(8,128)(2,1)} copy(bf16[1536,3072]{1,0:T(8,128)(2,1)} %param.8) | data formatting | bytes 18874368 | tf_op args[2]
  63.1 12.6 %copy.15 = bf16[1536,3072]{0,1:T(8,128)(2,1)} copy(bf16[1536,3072]{1,0:T(8,128)(2,1)} %param.9) | data formatting | bytes 18874368 | tf_op args[3]
  75.7 0.0 copy-done
  75.7 17.8 %fusion.18 = f32[2,1,3072]{2,1,0:T(1,128)S(1)} fusion(f32[2,1536,1]{1,0,2:T(2,128)S(1)} %bitcast.55, bf16[1,1536,3072]{1,2,0:T(8,128)(2,1)} %bitcast.61, bf16[1,1536,3072]{1,2,0:T(8,128)(2,1)} %bitcast.56), kind=kOutput, calls=%fused_computation.34 | convolution fusion | flops 122683392 | bytes 18911232 | tf_op jit(solution)/shard_map/kd,kdf->kf/dot_general | solution.py:22
  93.5 11.5 %psum.63 = f32[2,3072]{1,0:T(2,128)S(1)} all-reduce(f32[2,3072]{1,0:T(2,128)S(1)} %bitcast.67), channel_id=1, replica_groups=mesh['row'=4,'col'=8] {'row'}, use_global_device_ids=true, to_apply=%region_0.0 | all-reduce | flops 6144 | bytes 49152 | tf_op jit(solution)/shard_map/psum | solution.py:33
  105.0 10.8 %fusion.14 = f32[2,1,1536]{2,1,0:T(1,128)S(1)} fusion(f32[2,3072,1]{1,0,2:T(2,128)S(1)} %bitcast.73, bf16[1,1536,3072]{1,2,0:T(8,128)(2,1)} %bitcast.62, bf16[1,1536,3072]{1,2,0:T(8,128)(2,1)} %bitcast.57), kind=kOutput, calls=%fused_computation.25 | convolution fusion | flops 122683392 | bytes 18911232 | tf_op jit(solution)/shard_map/kdf,kf->kd/dot_general | solution.py:26
  115.9 36.8 %psum.64 = f32[2,1536]{1,0:T(2,128)S(1)} all-reduce(f32[2,1536]{1,0:T(2,128)S(1)} %bitcast.72), channel_id=1, replica_groups=mesh['row'=4,'col'=8] {'col'}, use_global_device_ids=true, to_apply=%region_1.0 | all-reduce | flops 3072 | bytes 24576 | tf_op jit(solution)/shard_map/psum | solution.py:34
  152.7 17.8 %fusion.16 = f32[2,1,3072]{2,1,0:T(1,128)S(1)} fusion(f32[2,1536,1]{1,0,2:T(2,128)S(1)} %bitcast.74, bf16[1,1536,3072]{1,2,0:T(8,128)(2,1)} %bitcast.63, bf16[1,1536,3072]{1,2,0:T(8,128)(2,1)} %bitcast.58), kind=kOutput, calls=%fused_computation.31 | convolution fusion | flops 122683392 | bytes 18911232 | tf_op jit(solution)/shard_map/kd,kdf->kf/dot_general | solution.py:22
  170.5 10.4 %psum.65 = f32[2,3072]{1,0:T(2,128)S(1)} all-reduce(f32[2,3072]{1,0:T(2,128)S(1)} %bitcast.68), channel_id=1, replica_groups=mesh['row'=4,'col'=8] {'row'}, use_global_device_ids=true, to_apply=%region_2.0 | all-reduce | flops 6144 | bytes 49152 | tf_op jit(solution)/shard_map/psum | solution.py:33
  181.0 10.8 %fusion.12 = f32[2,1,1536]{2,1,0:T(1,128)S(1)} fusion(f32[2,3072,1]{1,0,2:T(2,128)S(1)} %bitcast.66, bf16[1,1536,3072]{1,2,0:T(8,128)(2,1)} %bitcast.64, bf16[1,1536,3072]{1,2,0:T(8,128)(2,1)} %bitcast.59), kind=kOutput, calls=%fused_computation.22 | convolution fusion | flops 122683392 | bytes 18911232 | tf_op jit(solution)/shard_map/kdf,kf->kd/dot_general | solution.py:26
  191.8 0.1 multiply_reduce_fusion
  191.9 33.0 %all-reduce = (f32[2,1536]{1,0:T(2,128)S(1)}, f32[2]{0:T(128)S(1)}) all-reduce(f32[2,1536]{1,0:T(2,128)S(1)} %bitcast.71, f32[2]{0:T(128)S(1)} %multiply_reduce_fusion), channel_id=1, replica_groups=mesh['row'=4,'col'=8] {'col'}, use_global_device_ids=true, to_apply=%region_3.0 | all-reduce | flops 3074 | bytes 24592 | tf_op jit(solution)/shard_map/psum | solution.py:34
  224.9 0.1 multiply_reduce_fusion.1
  225.1 5.7 %psum.67 = f32[2]{0:T(128)S(1)} all-reduce(f32[2]{0:T(128)S(1)} %multiply_reduce_fusion.1), channel_id=1, replica_groups=mesh['row'=4,'col'=8] {'row'}, use_global_device_ids=true, to_apply=%region_5.0 | all-reduce | flops 2 | bytes 16 | tf_op jit(solution)/shard_map/psum | solution.py:37
  230.7 0.0 copy-done.9
  230.8 0.6 fusion.26
  231.4 0.0 all-reduce.4.cloned.1.call-done
  231.4 9.2 %fusion.23 = f32[256,1536]{1,0:T(8,128)} fusion(bf16[1536,3072]{1,0:T(8,128)(2,1)} %param.9, f32[256,3072]{1,0:T(8,128)} %all-reduce.4.cloned.1.call-done, f32[]{:T(128)} %bitcast.10), kind=kOutput, calls=%fused_computation.48 | convolution fusion | flops 2420637696 | bytes 14155780 | tf_op jit(solution)/shard_map/dot_general | solution.py:51
  240.5 0.0 reduce-scatter.3.cloned.1.call-update
  240.6 0.0 all-reduce.6.cloned.1.call-start
  240.6 0.1 broadcast_divide_fusion.1
  240.7 0.0 copy-start.8
  240.7 0.1 broadcast_divide_fusion
  240.8 0.0 copy-start.7
  240.8 20.8 %fusion.21 = f32[2,1536,3072]{1,2,0:T(8,128)} fusion(bf16[1,1536,3072]{1,2,0:T(8,128)(2,1)} %bitcast.65, bf16[1,1536,3072]{1,2,0:T(8,128)(2,1)} %bitcast.60), kind=kLoop, calls=%fused_computation.46 | loop fusion | flops 18874368 | bytes 56623104 | tf_op jit(solution)/shard_map/convert_element_type | solution.py:30
  261.6 41.5 %reduce-scatter.3.cloned.1.call-done = f32[32,1536]{1,0:T(8,128)} async-done(((f32[256,1536]{1,0:T(8,128)}), f32[32,1536]{1,0:T(8,128)}) %reduce-scatter.3.cloned.1.call-update) | async-done | bytes 196624 | tf_op jit(solution)/shard_map/reduce_scatter | solution.py:50
  303.1 0.0 copy-done.7
  303.1 1.6 multiply_convert_fusion.2
  304.7 32.0 %all_gather.7 = bf16[256,1536]{1,0:T(8,128)(2,1)S(1)} all-gather(bf16[32,1536]{1,0:T(8,128)(2,1)S(1)} %multiply_convert_fusion.2), channel_id=1, replica_groups=mesh['row'=4,'col'=8] {'col'}, dimensions={0}, use_global_device_ids=true | all-gather | bytes 884736 | tf_op jit(solution)/shard_map/all_gather | solution.py:60
  336.7 0.0 copy-start.6
  336.7 0.9 copy-done.6
  337.6 0.0 copy-start.2
  337.6 8.3 %fusion.28 = f32[256,3072]{1,0:T(8,128)} fusion(bf16[256,1536]{1,0:T(8,128)(2,1)S(1)} %all_gather.7, bf16[1536,3072]{1,0:T(8,128)(2,1)} %param.9), kind=kOutput, calls=%fused_computation.53 | convolution fusion | flops 2415919104 | bytes 13369344 | tf_op jit(solution)/shard_map/dot_general | solution.py:61
  345.9 0.0 all-reduce.6.cloned.1.call-update
  345.9 0.3 reduce-scatter.5.cloned.1.call-start
  346.2 0.0 copy-done.8
  346.3 0.0 copy-done.2
  346.3 9.8 %fusion.22 = f32[1536,3072]{1,0:T(8,128)} fusion(bf16[256,1536]{1,0:T(8,128)(2,1)} %copy-done.6, f32[256,3072]{1,0:T(8,128)S(1)} %copy-done.2, f32[]{:T(128)} %bitcast.10), kind=kOutput, calls=%fused_computation.47 | convolution fusion | flops 2420637696 | bytes 22806532 | tf_op jit(solution)/shard_map/dot_general | solution.py:67
  356.1 18.7 %copy.16 = f32[1536,3072]{0,1:T(8,128)} copy(f32[1536,3072]{1,0:T(8,128)} %fusion.22) | data formatting | bytes 37748736 | tf_op jit(solution)/shard_map/dot_general | solution.py:67
  374.8 38.7 %all-reduce.6.cloned.1.call-done = f32[256,3072]{1,0:T(8,128)} async-done(((f32[256,3072]{1,0:T(8,128)}), f32[256,3072]{1,0:T(8,128)}) %all-reduce.6.cloned.1.call-update) | async-done | bytes 3145744 | tf_op jit(solution)/shard_map/psum | solution.py:62
  413.5 4.3 fusion.11
  417.8 0.0 copy-start.3
  417.8 1.1 copy-done.3
  419.0 0.0 copy-start.5
  419.0 7.6 %fusion.29 = f32[256,1536]{1,0:T(8,128)} fusion(bf16[256,3072]{1,0:T(8,128)(2,1)S(1)} %fusion.11, bf16[1536,3072]{1,0:T(8,128)(2,1)} %param.8), kind=kOutput, calls=%fused_computation.54 | convolution fusion | flops 2415919104 | bytes 12582912 | tf_op jit(solution)/shard_map/dot_general | solution.py:79
  426.6 0.0 copy-done.5
  426.6 28.2 %fusion.3 = (f32[]{:T(128)}, f32[]{:T(128)}, f32[3072,1536]{1,0:T(8,128)}) fusion(f32[2,1536,3072]{1,2,0:T(8,128)} %fusion.21, f32[1536,3072]{0,1:T(8,128)} %copy.16, bf16[256,3072]{1,0:T(8,128)(2,1)} %copy-done.3, bf16[256,1536]{1,0:T(8,128)(2,1)S(1)} %copy-done.5), kind=kOutput, calls=%fused_computation.5 | convolution fusion | flops 2434793472 | bytes 77856776 | tf_op jit(solution)/shard_map/dot_general | solution.py:64
  454.8 1.4 pad_maximum_fusion.1
  456.1 0.0 reduce-scatter.5.cloned.1.call-update
  456.2 40.1 %psum.71 = f32[2]{0:T(128)S(1)} all-reduce(f32[2]{0:T(128)S(1)} %pad_maximum_fusion.1), channel_id=1, replica_groups=mesh['row'=4,'col'=8] {'row','col'}, use_global_device_ids=true, to_apply=%region_14.0 | all-reduce | flops 2 | bytes 16 | tf_op jit(solution)/shard_map/psum | solution.py:71
  496.3 0.6 fusion.25
  496.9 13.9 %fusion.5 = bf16[1536,3072]{0,1:T(8,128)(2,1)} fusion(f32[3072,1536]{1,0:T(8,128)} %get-tuple-element.27, f32[3072]{0:T(1024)S(1)} %bitcast.70, f32[1536]{0:T(1024)S(1)} %get-tuple-element.15, f32[]{:T(128)} %bitcast.17, f32[]{:T(128)} %bitcast.10), kind=kLoop, calls=%fused_computation.9 | loop fusion | flops 23592960 | bytes 28329992 | tf_op jit(solution)/shard_map/convert_element_type | solution.py:88
  510.8 12.6 %copy.17 = bf16[1536,3072]{1,0:T(8,128)(2,1)} copy(bf16[1536,3072]{0,1:T(8,128)(2,1)} %fusion.5) | data formatting | bytes 18874368
  523.4 13.9 %subtract_convert_fusion = bf16[1536,3072]{1,0:T(8,128)(2,1)} fusion(f32[1536,3072]{1,0:T(8,128)} %fusion.22, f32[3072]{0:T(1024)S(1)} %bitcast.69, f32[1536]{0:T(1024)S(1)} %get-tuple-element.14, f32[]{:T(128)} %bitcast.19, f32[]{:T(128)} %bitcast.11), kind=kLoop, calls=%fused_computation.10 | loop fusion | flops 23592960 | bytes 28329992 | tf_op jit(solution)/shard_map/convert_element_type | solution.py:89
  537.3 2.3 multiply_convert_fusion.1
  539.6 0.0 copy-done.1
  (12 shorter events, 0.1 us)
Async XLA Ops:
  7.2 68.5 %copy-start = (f32[2,1536]{1,0:T(2,128)S(1)}, f32[2,1536]{1,0:T(2,128)}, u32[]{:S(2)}) copy-start(f32[2,1536]{1,0:T(2,128)} %param.11) | copy-start | bytes 36868
  7.2 224.2 %all-reduce.4.cloned.1.call-start = ((), (), s32[]{:S(2)}) async-start(), calls=%async_computation.2 | async-start | bytes 6291456 | tf_op jit(solution)/shard_map/psum | solution.py:46
  41.3 0.9 copy-start.4
  50.3 252.8 %reduce-scatter.3.cloned.1.call-start = ((), (), s32[]{:S(2)}) async-start(), calls=%async_computation.3 | async-start | bytes 1769472 | tf_op jit(solution)/shard_map/reduce_scatter | solution.py:50
  181.0 49.7 %copy-start.9 = (f32[2]{0:T(128)S(1)}, f32[2]{0:T(128)}, u32[]{:S(2)}) copy-start(f32[2]{0:T(128)} %param.10) | copy-start | bytes 28
  240.6 172.9 %all-reduce.6.cloned.1.call-start = ((), (), s32[]{:S(2)}) async-start(), calls=%async_computation.4 | async-start | bytes 6291456 | tf_op jit(solution)/shard_map/psum | solution.py:62
  240.7 105.5 %copy-start.8 = (f32[2,1536]{1,0:T(2,128)}, f32[2,1536]{1,0:T(2,128)S(1)}, u32[]{:S(2)}) copy-start(f32[2,1536]{1,0:T(2,128)S(1)} %broadcast_divide_fusion.1) | copy-start | bytes 36868
  240.8 62.3 %copy-start.7 = (bf16[32,1536]{1,0:T(8,128)(2,1)S(1)}, bf16[32,1536]{1,0:T(8,128)(2,1)}, u32[]{:S(2)}) copy-start(bf16[32,1536]{1,0:T(8,128)(2,1)} %param.7) | copy-start | bytes 294916
  336.7 0.9 copy-start.6
  337.6 8.6 %copy-start.2 = (f32[256,3072]{1,0:T(8,128)S(1)}, f32[256,3072]{1,0:T(8,128)}, u32[]{:S(2)}) copy-start(f32[256,3072]{1,0:T(8,128)} %all-reduce.4.cloned.1.call-done) | copy-start | bytes 9437188
  345.9 191.4 %reduce-scatter.5.cloned.1.call-start = ((), (), s32[]{:S(2)}) async-start(), calls=%async_computation.5 | async-start | bytes 1769472 | tf_op jit(solution)/shard_map/reduce_scatter | solution.py:78
  417.8 1.1 copy-start.3
  419.0 7.6 %copy-start.5 = (bf16[256,1536]{1,0:T(8,128)(2,1)S(1)}, bf16[256,1536]{1,0:T(8,128)(2,1)}, u32[]{:S(2)}) copy-start(bf16[256,1536]{1,0:T(8,128)(2,1)} %copy-done.4) | copy-start | bytes 2359300
  523.4 16.2 %copy-start.1 = (f32[2,1536]{1,0:T(2,128)S(1)}, f32[2,1536]{1,0:T(2,128)}, u32[]{:S(2)}) copy-start(f32[2,1536]{1,0:T(2,128)} %param.11) | copy-start | bytes 36868
Sparse Core Ops, SparseCore 0:
  50.4 69.8 all-reduce.3
  240.7 62.3 reduce-scatter.2
  346.0 67.4 all-reduce.5
  456.3 65.5 reduce-scatter.4
where the time goes:
time: 548 us; the launch traced here: 546 us
  blocking collectives  204 us (37%)
  matrix products  128 us (23%)
  waiting for transfers between devices  80.2 us (15%)
  local copies, waits for them, and re-layouts  60.9 us (11%)
  other arithmetic  58.6 us (11%)
  between operations  13.9 us (3%)
    psum x2, blocking collectives, shards(): lax.psum((times_right(weights, right_vec), jnp.sum(right_vec * right_vec,...  69.8 us
    reduce_scatter x1, waiting for transfers between devices, shards(): lax.psum_scatter(lax.dot_general(block_rows, w_out, (((1,), (1,)), ((), (...  41.5 us
    unnamed x23, local copies, waits for them, and re-layouts  40.9 us
    psum x1, blocking collectives, shards(): traces = lax.psum(local_traces, ('row', 'col'))  40.1 us
    psum x1, waiting for transfers between devices, shards(): delta = scales[1] * lax.psum(partial_delta, 'row')  38.7 us
    dot_general x2, matrix products, times_left(): jnp.einsum('kd,kdf->kf', current, weights, precision=lax.Precision.HIGHEST)  35.6 us
    all_gather x1, blocking collectives, shards(): token_all = lax.all_gather(tokens, 'col', axis=0, tiled=True)  34 us
    all_gather x1, blocking collectives, shards(): grad_all = lax.all_gather(grad_output, 'col', axis=0, tiled=True)  32 us
  transfers between devices with their start and end apart: 4, of which 2 were waited for; matrix products, arithmetic and copies ran while one was open for 32% of the time, Pallas kernels for 0%

commit v1 on v0

v1 whole, which is shorter than its diff:
```python
import functools

import jax
import jax.numpy as jnp
from jax import lax
from jax.experimental import pallas as pl
from jax.experimental.pallas import tpu as pltpu
from jax.sharding import PartitionSpec as P

POWER = 2
EPSILON = 1e-06
ROOT_HALF = 0.7071067811865476
INV_ROOT_TWO_PI = 0.3989422804014327
BF16 = jnp.bfloat16
F32 = jnp.float32
MESH = pl.DeviceIdType.MESH
LANES = 128


def tile_of(n):
    return 512 if n % 512 == 0 else 256


def pieces(vec):
    high = vec.astype(BF16).astype(F32)
    rest = vec - high
    mid = rest.astype(BF16).astype(F32)
    low = rest - mid
    row = lax.broadcasted_iota(jnp.int32, (16, vec.shape[1]), 0)
    stacked = jnp.where(row == 0, high, jnp.where(row == 1, mid, jnp.where(row == 2, low, 0.0)))
    return stacked.astype(BF16)


def body(
    rows_n, cols_n,
    tokens, target, gains, u_start, w_in_hbm, w_out_hbm,
    tok_all, act_all, g_all, gh_all, u_next, v_units, coeffs, grad_tokens,
    w_in, w_out, part, slopes, hid, own, s1, r1, s2, r2, outp, so, ro, pieces_l, pieces_r,
    uvec, left, right, p_buf, q_buf, n_buf, tr_buf, tc_buf,
    w_sem, out_sem,
    tok_s, tok_r, p_s, p_r, q_s, q_r, n_s, n_r, tr_s, tr_r, tc_s, tc_r,
    s1_s, s1_r, s2_s, s2_r, ag_s, ag_r, fw_s, fw_r, ro_s, ro_r, g_s, g_r,
):
    del out_sem
    row, col = lax.axis_index("row"), lax.axis_index("col")
    ys = rows_n // 2
    y, core = row // 2, row % 2
    mate = y * 2 + (1 - core)
    depth, width = w_in.shape
    total = tok_all.shape[0]
    block = total // cols_n
    chunk = total // rows_n

    loads = [
        pltpu.make_async_copy(w_in_hbm, w_in, w_sem.at[0]),
        pltpu.make_async_copy(w_out_hbm, w_out, w_sem.at[1]),
    ]
    for load in loads:
        load.start()

    barrier = pltpu.get_barrier_semaphore()
    for i in range(1, rows_n):
        pl.semaphore_signal(
            barrier, inc=1, device_id=((row + i) % rows_n, col), device_id_type=MESH
        )
    for i in range(1, cols_n):
        pl.semaphore_signal(
            barrier, inc=1, device_id=(row, (col + i) % cols_n), device_id_type=MESH
        )
    pl.semaphore_wait(barrier, rows_n + cols_n - 2)

    def remote(src, dst, send, recv, dev):
        return pltpu.make_async_remote_copy(
            src_ref=src, dst_ref=dst, send_sem=send, recv_sem=recv, device_id=dev,
            device_id_type=MESH,
        )

    def row_send(buf, send, recv):
        copies = []
        for i in range(1, rows_n):
            c = remote(buf.at[row], buf.at[row], send.at[i], recv.at[i],
                       ((row + i) % rows_n, col))
            c.start()
            copies.append(c)
        return copies

    def col_send(buf, send, recv):
        copies = []
        for i in range(1, cols_n):
            c = remote(buf.at[col], buf.at[col], send.at[i], recv.at[i],
                       (row, (col + i) % cols_n))
            c.start()
            copies.append(c)
        return copies

    def wait_all(copies):
        for c in copies:
            c.wait()

    def slot_sum(buf, n):
        acc = buf[0]
        for j in range(1, n):
            acc = acc + buf[j]
        return acc

    my_rows = pl.ds(pl.multiple_of(col * block, block), block)
    tok_all[my_rows, :] = tokens[...]
    tok_copies = []
    for i in range(1, cols_n):
        c = remote(tokens, tok_all.at[my_rows, :], tok_s.at[i], tok_r.at[i],
                   (row, (col + i) % cols_n))
        c.start()
        tok_copies.append(c)

    weights = (w_in, w_out)

    def times_left(k, vec):
        pieces_l[...] = pieces(vec)
        t = tile_of(width)

        def step(i, _):
            cs = pl.ds(pl.multiple_of(i * t, t), t)
            out = jnp.dot(pieces_l[...], weights[k][:, cs], preferred_element_type=F32)
            left[k : k + 1, cs] = jnp.sum(out, axis=0, keepdims=True)
            return 0

        lax.fori_loop(0, width // t, step, 0)

    def times_right(k, vec):
        pieces_r[...] = pieces(vec)
        t = 256

        def step(i, _):
            rs = pl.ds(pl.multiple_of(i * t, t), t)
            out = lax.dot_general(
                pieces_r[...], weights[k][rs, :], (((1,), (1,)), ((), ())),
                preferred_element_type=F32,
            )
            right[k : k + 1, rs] = jnp.sum(out, axis=0, keepdims=True)
            return 0

        lax.fori_loop(0, depth // t, step, 0)

    def matmul_nn(a, w):
        t = tile_of(width)

        def step(i, _):
            cs = pl.ds(pl.multiple_of(i * t, t), t)
            part[:, cs] = jnp.dot(a[...], w[:, cs], preferred_element_type=F32)
            return 0

        lax.fori_loop(0, width // t, step, 0)

    def matmul_nt(a, w):
        t = 256

        def step(i, _):
            cs = pl.ds(pl.multiple_of(i * t, t), t)
            outp[:, cs] = lax.dot_general(
                a[...], w[cs, :], (((1,), (1,)), ((), ())), preferred_element_type=F32
            )
            return 0

        lax.fori_loop(0, depth // t, step, 0)

    def rows_of(yy, cc):
        return pl.ds(pl.multiple_of((yy * 2 + cc) * chunk, chunk), chunk)

    def reduce_first(e):
        copies = []
        for yy in range(ys):
            s1[e, yy] = part[rows_of(yy, 1 - core), :].astype(BF16)
            c = remote(s1.at[e, yy], r1.at[e, yy], s1_s.at[e, yy], s1_r.at[e, yy], (mate, col))
            c.start()
            copies.append(c)
        return copies

    def reduce_second(e, first):
        wait_all(first)
        copies = []
        for i in range(1, ys):
            other = (y + i) % ys
            s2[e, i] = (part[rows_of(other, core), :] + r1[e, other].astype(F32)).astype(BF16)
            c = remote(s2.at[e, i], r2.at[e, i], s2_s.at[e, i], s2_r.at[e, i],
                       (other * 2 + core, col))
            c.start()
            copies.append(c)
        own[...] = part[rows_of(y, core), :] + r1[e, y].astype(F32)
        return copies

    def reduce_last(e, copies):
        wait_all(copies)
        acc = own[...]
        for i in range(1, ys):
            acc = acc + r2[e, i].astype(F32)
        return acc

    def gather_rows(e, buf):
        mine = rows_of(y, core)
        copies = []
        for i in range(1, ys):
            c = remote(buf.at[mine, :], buf.at[mine, :], ag_s.at[e, i], ag_r.at[e, i],
                       (((y + i) % ys) * 2 + core, col))
            c.start()
            copies.append(c)
        c = remote(buf.at[mine, :], buf.at[mine, :], fw_s.at[e, 0], fw_r.at[e, 0], (mate, col))
        c.start()
        return copies, [c]

    def gather_finish(e, buf, state):
        copies, forwards = state
        for i in range(1, ys):
            copies[i - 1].wait_recv()
            got = rows_of((y + ys - i) % ys, core)
            f = remote(buf.at[got, :], buf.at[got, :], fw_s.at[e, i], fw_r.at[e, i], (mate, col))
            f.start()
            forwards.append(f)
        for c in copies:
            c.wait_send()
        wait_all(forwards)

    def scatter_cols(e):
        copies = []
        for i in range(1, cols_n):
            other = (col + i) % cols_n
            rs = pl.ds(pl.multiple_of(other * block, block), block)
            so[e, i] = outp[rs, :].astype(BF16)
            c = remote(so.at[e, i], ro.at[e, i], ro_s.at[e, i], ro_r.at[e, i], (row, other))
            c.start()
            copies.append(c)
        return copies

    def scatter_finish(e, copies):
        acc = outp[my_rows, :]
        for i in range(1, cols_n):
            copies[i - 1].wait()
            acc = acc + ro[e, i].astype(F32)
        return acc

    def send_left(it, squares):
        p_buf[it, row, :, :width] = left[...]
        p_buf[it, row, :, width:] = jnp.broadcast_to(squares, (2, LANES))
        return row_send(p_buf.at[it], p_s.at[it], p_r.at[it])

    def send_right(it, squares):
        q_buf[it, col, :, :depth] = right[...]
        q_buf[it, col, :, depth:] = jnp.broadcast_to(squares, (2, LANES))
        return col_send(q_buf.at[it], q_s.at[it], q_r.at[it])

    def square_sum(vec):
        return jnp.sum(vec * vec, axis=1, keepdims=True)

    uvec[...] = u_start[...]
    loads[0].wait()
    times_left(0, uvec[0:1, :])
    loads[1].wait()
    times_left(1, uvec[1:2, :])
    p_copies = send_left(0, jnp.zeros((2, 1), F32))

    wait_all(tok_copies)
    matmul_nn(tok_all, w_in)
    first = reduce_first(0)

    wait_all(p_copies)
    left[...] = slot_sum(p_buf.at[0], rows_n)[:, :width]
    times_right(0, left[0:1, :])
    times_right(1, left[1:2, :])
    q_copies = send_right(0, square_sum(left[...]))

    second = reduce_second(0, first)

    wait_all(q_copies)
    summed = slot_sum(q_buf.at[0], cols_n)
    norm = jnp.sqrt(summed[:, depth : depth + 1] + EPSILON)
    uvec[...] = summed[:, :depth] / norm
    squares = square_sum(uvec[...])
    times_left(0, uvec[0:1, :])
    times_left(1, uvec[1:2, :])
    p_copies = send_left(1, squares)

    hid[...] = reduce_last(0, second)

    wait_all(p_copies)
    summed = slot_sum(p_buf.at[1], rows_n)
    sigma = jnp.sqrt(summed[:, width : width + 1] + EPSILON)
    left[...] = summed[:, :width] / sigma
    times_right(0, left[0:1, :])
    times_right(1, left[1:2, :])
    q_copies = send_right(1, square_sum(left[...]))
    wait_all(q_copies)
    summed = slot_sum(q_buf.at[1], cols_n)
    norm = jnp.sqrt(summed[:, depth : depth + 1] + EPSILON)
    v_units[...] = left[...] / norm
    uvec[...] = summed[:, :depth] / norm
    n_buf[row] = jnp.broadcast_to(square_sum(uvec[...]), (2, LANES))
    wait_all(row_send(n_buf, n_s, n_r))
    sigma = jnp.sqrt(slot_sum(n_buf, rows_n)[:, 0:1] + EPSILON)
    u_next[...] = uvec[...] / sigma
    scales = gains[:, 0:1] / sigma
    scale_in, scale_out = scales[0:1, :], scales[1:2, :]

    base = row * chunk

    def act_step(i, _):
        rs = pl.ds(pl.multiple_of(i * 16, 16), 16)
        h = hid[rs, :] * scale_in
        cdf = 0.5 * (1.0 + lax.erf(h * ROOT_HALF))
        slopes[rs, :] = cdf + h * jnp.exp(-0.5 * h * h) * INV_ROOT_TWO_PI
        act_all[pl.ds(pl.multiple_of(base + i * 16, 16), 16), :] = (h * cdf).astype(BF16)
        return 0

    lax.fori_loop(0, chunk // 16, act_step, 0)
    gather_finish(0, act_all, gather_rows(0, act_all))

    matmul_nt(act_all, w_out)
    output = scale_out * scatter_finish(0, scatter_cols(0))
    loss_scale = 1.0 / jnp.sqrt(jnp.float32(total))
    g_all[my_rows, :] = ((output - target[...].astype(F32)) * loss_scale).astype(BF16)
    g_copies = []
    for i in range(1, cols_n):
        c = remote(g_all.at[my_rows, :], g_all.at[my_rows, :], g_s.at[i], g_r.at[i],
                   (row, (col + i) % cols_n))
        c.start()
        g_copies.append(c)
    wait_all(g_copies)

    matmul_nn(g_all, w_out)
    own[...] = reduce_last(1, reduce_second(1, reduce_first(1)))

    def grad_step(i, sums):
        rs = pl.ds(pl.multiple_of(i * 16, 16), 16)
        ra = pl.ds(pl.multiple_of(base + i * 16, 16), 16)
        d = own[rs, :]
        grad = (scale_out * d * slopes[rs, :]).astype(BF16)
        gh_all[ra, :] = grad
        a = jnp.sum(grad.astype(F32) * hid[rs, :], axis=0, keepdims=True)
        b = jnp.sum(act_all[ra, :].astype(F32) * d, axis=0, keepdims=True)
        return sums[0] + a, sums[1] + b

    zero = jnp.zeros((1, width), F32)
    sum_in, sum_out = lax.fori_loop(0, chunk // 16, grad_step, (zero, zero))
    state = gather_rows(1, gh_all)
    tr_buf[row, 0:1] = jnp.broadcast_to(jnp.sum(sum_in, axis=1, keepdims=True), (1, LANES))
    tr_buf[row, 1:2] = jnp.broadcast_to(jnp.sum(sum_out, axis=1, keepdims=True), (1, LANES))
    wait_all(row_send(tr_buf, tr_s, tr_r))
    tc_buf[col] = slot_sum(tr_buf, rows_n)
    tc_copies = col_send(tc_buf, tc_s, tc_r)
    gather_finish(1, gh_all, state)

    matmul_nt(gh_all, w_in)
    copies = scatter_cols(1)
    wait_all(tc_copies)
    traces = slot_sum(tc_buf, cols_n)
    coeffs[0:2, :] = jnp.broadcast_to(scales, (2, LANES))
    coeffs[2:4, :] = scales * traces / sigma
    grad_tokens[...] = (scale_in * scatter_finish(1, copies)).astype(BF16)


def shards(rows_n, cols_n, tokens, target, w_in, w_out, gains, u_start):
    block, depth = tokens.shape
    width = w_in.shape[1]
    total = block * cols_n
    ys = rows_n // 2
    chunk = total // rows_n
    vmem = pl.BlockSpec(memory_space=pltpu.VMEM)
    dma = pltpu.SemaphoreType.DMA
    S = pltpu.VMEM
    wide_gains = jnp.broadcast_to(gains[:, None], (2, LANES))
    tok_all, act_all, g_all, gh_all, u_next, v_units, coeffs, grad_tokens = pl.pallas_call(
        functools.partial(body, rows_n, cols_n),
        out_shape=(
            jax.ShapeDtypeStruct((total, depth), BF16),
            jax.ShapeDtypeStruct((total, width), BF16),
            jax.ShapeDtypeStruct((total, depth), BF16),
            jax.ShapeDtypeStruct((total, width), BF16),
            jax.ShapeDtypeStruct((2, depth), F32),
            jax.ShapeDtypeStruct((2, width), F32),
            jax.ShapeDtypeStruct((4, LANES), F32),
            jax.ShapeDtypeStruct((block, depth), BF16),
        ),
        in_specs=[vmem] * 4 + [pl.BlockSpec(memory_space=pl.ANY)] * 2,
        out_specs=[vmem] * 8,
        scratch_shapes=[
            S((depth, width), BF16), S((depth, width), BF16),
            S((total, width), F32),
            S((chunk, width), F32), S((chunk, width), F32), S((chunk, width), F32),
            S((2, ys, chunk, width), BF16), S((2, ys, chunk, width), BF16),
            S((2, ys, chunk, width), BF16), S((2, ys, chunk, width), BF16),
            S((total, depth), F32),
            S((2, cols_n, block, depth), BF16), S((2, cols_n, block, depth), BF16),
            S((16, depth), BF16), S((16, width), BF16),
            S((2, depth), F32), S((2, width), F32), S((2, depth), F32),
            S((2, rows_n, 2, width + LANES), F32),
            S((2, cols_n, 2, depth + LANES), F32),
            S((rows_n, 2, LANES), F32), S((rows_n, 2, LANES), F32), S((cols_n, 2, LANES), F32),
            dma((2,)), dma((2,)),
            dma((cols_n,)), dma((cols_n,)),
            dma((2, rows_n)), dma((2, rows_n)),
            dma((2, cols_n)), dma((2, cols_n)),
            dma((rows_n,)), dma((rows_n,)),
            dma((rows_n,)), dma((rows_n,)),
            dma((cols_n,)), dma((cols_n,)),
            dma((2, ys)), dma((2, ys)),
            dma((2, ys)), dma((2, ys)),
            dma((2, ys)), dma((2, ys)),
            dma((2, ys)), dma((2, ys)),
            dma((2, cols_n)), dma((2, cols_n)),
            dma((cols_n,)), dma((cols_n,)),
        ],
        compiler_params=pltpu.CompilerParams(
            collective_id=0, has_side_effects=True, vmem_limit_bytes=58 * 1024 * 1024
        ),
    )(tokens, target, wide_gains, u_start, w_in, w_out)
    block_in = lax.dot_general(
        tok_all, gh_all, (((0,), (0,)), ((), ())), preferred_element_type=F32
    )
    block_out = lax.dot_general(
        g_all, act_all, (((0,), (0,)), ((), ())), preferred_element_type=F32
    )
    grad_in = coeffs[0, 0] * block_in - coeffs[2, 0] * (u_next[0][:, None] * v_units[0][None, :])
    grad_out = coeffs[1, 0] * block_out - coeffs[3, 0] * (
        u_next[1][:, None] * v_units[1][None, :]
    )
    return grad_tokens, grad_in.astype(BF16), grad_out.astype(BF16), u_next


def solution(mesh):
    placed = (
        P("col", "row"),
        P("col", "row"),
        P("row", "col"),
        P("row", "col"),
        P(),
        P(None, "row"),
    )
    return jax.shard_map(
        functools.partial(shards, mesh.shape["row"], mesh.shape["col"]),
        mesh=mesh,
        in_specs=placed,
        out_specs=(P("col", "row"), P("row", "col"), P("row", "col"), P(None, "row")),
        check_vma=False,
    )
```

time: 548 us -> 190 us (0.35)
  the two profiles are of different devices: /device:TPU:0 before, /device:TPU:26 now
where the time goes in v1:
time: 190 us; the launch traced here: 189 us
  Pallas kernels  165 us (87%)
  matrix products  17.8 us (9%)
  local copies, waits for them, and re-layouts  5.62 us (3%)
    pallas_call x1, Pallas kernels, shards(): pl.pallas_call(functools.partial(body, rows_n, cols_n), out_shape=(jax.Sh...  165 us
    dot_general x1, matrix products, shards(): lax.dot_general(tok_all, gh_all, (((0,), (0,)), ((), ())), preferred_elem...  10.4 us
    dot_general x1, matrix products, shards(): lax.dot_general(g_all, act_all, (((0,), (0,)), ((), ())), preferred_eleme...  7.38 us

profile of v1, /device:TPU:26, one launch (start us, length us, event | category | flops | bytes accessed | tf_op | source)
XLA Modules:
  0.0 189.5 jit_solution(1503515357844594223)
XLA Ops:
  0.6 1.3 broadcast_in_dim.2.gains
  1.9 165.4 %shard_map.93 = (bf16[256,1536]{1,0:T(8,128)(2,1)}, bf16[256,3072]{1,0:T(8,128)(2,1)}, bf16[256,1536]{1,0:T(8,128)(2,1)}, bf16[256,3072]{1,0:T(8,128)(2,1)}, f32...) custom-call(bf16[32,1536]{1,0:T(8,128)(2,1)} %tokens.1, ...), custom_call_target="tpu_custom_call" | custom-call | tf_op jit(solution)/shard_map/pallas_call | solution.py:369
  167.3 1.4 fusion.1
  168.7 0.8 slice_reduce_fusion
  169.6 0.8 fusion
  170.4 0.0 copy-start.2
  170.4 0.0 copy-start.3
  170.4 10.4 %subtract_convert_fusion.1 = bf16[1536,3072]{1,0:T(8,128)(2,1)} fusion(bf16[256,1536]{1,0:T(8,128)(2,1)} %get-tuple-element.14, bf16[256,3072]{1,0:T(8,128)(2,1)} %get-tuple-element.15, f32[3072]{0:T(1024)S(1)} %bitcast.11, f32[1536]{0:T(1024)S(1)} %get-tuple-element.21, f32[]{:T(128)} %bitcast.1, f32[]{:T(128)} %bitcast), kind=kOutput, calls=%fused_computation.1 | convolution fusion | flops 2439512064 | bytes 11814920 | tf_op jit(solution)/shard_map/dot_general | solution.py:414
  180.8 0.0 copy-done.2
  180.8 0.0 copy-done.3
  180.8 0.0 copy-start
  180.9 0.0 copy-start.1
  180.9 7.4 %subtract_convert_fusion = bf16[1536,3072]{1,0:T(8,128)(2,1)} fusion(bf16[256,1536]{1,0:T(8,128)(2,1)S(1)} %copy-done.3, bf16[256,3072]{1,0:T(8,128)(2,1)S(1)} %copy-done.2, f32[3072]{0:T(1024)S(1)} %bitcast.10, f32[1536]{0:T(1024)S(1)} %get-tuple-element.20, f32[]{:T(128)} %bitcast.4, f32[]{:T(128)} %bitcast.3), kind=kOutput, calls=%fused_computation | convolution fusion | flops 2439512064 | bytes 11814920 | tf_op jit(solution)/shard_map/dot_general | solution.py:417
  188.2 0.0 copy-done
  188.2 0.6 copy.12
  188.9 0.0 copy-done.1
  188.9 0.6 copy.13
Async XLA Ops:
  170.4 10.4 %copy-start.2 = (bf16[256,3072]{1,0:T(8,128)(2,1)S(1)}, bf16[256,3072]{1,0:T(8,128)(2,1)}, u32[]{:S(2)}) copy-start(bf16[256,3072]{1,0:T(8,128)(2,1)} %get-tuple-element.19) | copy-start | bytes 4718596
  170.4 10.4 %copy-start.3 = (bf16[256,1536]{1,0:T(8,128)(2,1)S(1)}, bf16[256,1536]{1,0:T(8,128)(2,1)}, u32[]{:S(2)}) copy-start(bf16[256,1536]{1,0:T(8,128)(2,1)} %get-tuple-element.18) | copy-start | bytes 2359300
  180.8 7.4 %copy-start = (bf16[32,1536]{1,0:T(8,128)(2,1)S(1)}, bf16[32,1536]{1,0:T(8,128)(2,1)}, u32[]{:S(2)}) copy-start(bf16[32,1536]{1,0:T(8,128)(2,1)} %get-tuple-element.32) | copy-start | bytes 294916
  180.9 8.0 %copy-start.1 = (f32[2,1536]{1,0:T(2,128)S(1)}, f32[2,1536]{1,0:T(2,128)}, u32[]{:S(2)}) copy-start(f32[2,1536]{1,0:T(2,128)} %get-tuple-element.35) | copy-start | bytes 36868

commit v2 on v1

v2 whole, which is shorter than its diff:
```python
import functools

import jax
import jax.numpy as jnp
from jax import lax
from jax.experimental import pallas as pl
from jax.experimental.pallas import tpu as pltpu
from jax.sharding import PartitionSpec as P

POWER = 2
EPSILON = 1e-06
ROOT_HALF = 0.7071067811865476
INV_ROOT_TWO_PI = 0.3989422804014327
BF16 = jnp.bfloat16
F32 = jnp.float32
MESH = pl.DeviceIdType.MESH
LANES = 128


PARTS = 2


def tile_of(n):
    for t in (512, 256, 384):
        if n % t == 0:
            return t
    return LANES


def pieces(vec):
    high = vec.astype(BF16).astype(F32)
    rest = vec - high
    mid = rest.astype(BF16).astype(F32)
    low = rest - mid
    row = lax.broadcasted_iota(jnp.int32, (16, vec.shape[1]), 0)
    stacked = jnp.where(row == 0, high, jnp.where(row == 1, mid, jnp.where(row == 2, low, 0.0)))
    return stacked.astype(BF16)


def body(
    rows_n, cols_n,
    tokens, target, gains, u_start, w_in_hbm, w_out_hbm,
    tok_all, act_all, g_all, gh_all, u_next, v_units, coeffs, grad_tokens,
    w_in, w_out, part, slopes, hid, own, rs1, rr1, rs2, rr2, outp, out_own, cs1, cr1, cs2, cr2,
    pieces_l, pieces_r, left, right, p_buf, q_buf, n_buf, tr_buf, tc_buf,
    w_sem, p_s, p_r, q_s, q_r, n_s, n_r, tr_s, tr_r, tc_s, tc_r,
    rs1_s, rs1_r, rs2_s, rs2_r, cs1_s, cs1_r, cs2_s, cs2_r,
    rg_s, rg_r, rf_s, rf_r, cg_s, cg_r, cf_s, cf_r,
):
    row, col = lax.axis_index("row"), lax.axis_index("col")
    depth, width = w_in.shape
    total = tok_all.shape[0]
    block = total // cols_n
    chunk = total // rows_n

    loads = [
        pltpu.make_async_copy(w_in_hbm, w_in, w_sem.at[0]),
        pltpu.make_async_copy(w_out_hbm, w_out, w_sem.at[1]),
    ]
    for load in loads:
        load.start()

    def on_row(i):
        return (i, col)

    def on_col(i):
        return (row, i)

    barrier = pltpu.get_barrier_semaphore()
    for i in range(1, rows_n):
        pl.semaphore_signal(
            barrier, inc=1, device_id=on_row((row + i) % rows_n), device_id_type=MESH
        )
    for i in range(1, cols_n):
        pl.semaphore_signal(
            barrier, inc=1, device_id=on_col((col + i) % cols_n), device_id_type=MESH
        )
    pl.semaphore_wait(barrier, rows_n + cols_n - 2)

    def remote(src, dst, send, recv, dev):
        return pltpu.make_async_remote_copy(
            src_ref=src, dst_ref=dst, send_sem=send, recv_sem=recv, device_id=dev,
            device_id_type=MESH,
        )

    def all_send(n, me, dev, buf, send, recv):
        copies = []
        for i in range(1, n):
            c = remote(buf.at[me], buf.at[me], send.at[i], recv.at[i], dev((me + i) % n))
            c.start()
            copies.append(c)
        return copies

    row_send = functools.partial(all_send, rows_n, row, on_row)
    col_send = functools.partial(all_send, cols_n, col, on_col)

    def wait_all(copies):
        for c in copies:
            c.wait()

    def slot_sum(buf, n):
        acc = buf[0]
        for j in range(1, n):
            acc = acc + buf[j]
        return acc

    class Axis:
        def __init__(self, n, me, dev, size, bufs, sems, gather_sems):
            self.count, self.size, self.dev = n // 2, size, dev
            self.high, self.low = me // 2, me % 2
            self.mate = dev(self.high * 2 + 1 - self.low)
            self.bufs, self.sems, self.gather_sems = bufs, sems, gather_sems

        def rows(self, high, low):
            return pl.ds(pl.multiple_of((high * 2 + low) * self.size, self.size), self.size)

        def first(self, e, h, src):
            s1, r1 = self.bufs[:2]
            s_s, s_r = self.sems[:2]
            cols = half(src.shape[1], h)
            copies = []
            for i in range(1, self.count + 1):
                other = (self.high + i) % self.count
                s1[e, h, i - 1] = src[self.rows(other, 1 - self.low), cols].astype(BF16)
                c = remote(s1.at[e, h, i - 1], r1.at[e, h, i - 1], s_s.at[e, h, i - 1],
                           s_r.at[e, h, i - 1], self.mate)
                c.start()
                copies.append(c)
            return copies

        def second(self, e, h, src, dst, copies):
            s2, r2 = self.bufs[2:]
            r1 = self.bufs[1]
            s_s, s_r = self.sems[2:]
            cols = half(src.shape[1], h)
            sent = []
            for i in range(1, self.count):
                copies[i - 1].wait()
                other = (self.high + i) % self.count
                s2[e, h, i - 1] = (
                    src[self.rows(other, self.low), cols] + r1[e, h, i - 1].astype(F32)
                ).astype(BF16)
                c = remote(s2.at[e, h, i - 1], r2.at[e, h, i - 1], s_s.at[e, h, i - 1],
                           s_r.at[e, h, i - 1], self.dev(other * 2 + self.low))
                c.start()
                sent.append(c)
            copies[-1].wait()
            dst[:, cols] = (
                src[self.rows(self.high, self.low), cols]
                + r1[e, h, self.count - 1].astype(F32)
            )
            return sent

        def last(self, e, h, dst, sent):
            r2 = self.bufs[3]
            cols = half(dst.shape[1], h)
            wait_all(sent)
            acc = dst[:, cols]
            for i in range(1, self.count):
                acc = acc + r2[e, h, i - 1].astype(F32)
            dst[:, cols] = acc

        def gather(self, e, buf):
            g_s, g_r, f_s, f_r = self.gather_sems
            mine = buf.at[self.rows(self.high, self.low), :]
            copies = []
            for i in range(1, self.count):
                c = remote(mine, mine, g_s.at[e, i], g_r.at[e, i],
                           self.dev(((self.high + i) % self.count) * 2 + self.low))
                c.start()
                copies.append(c)
            c = remote(mine, mine, f_s.at[e, 0], f_r.at[e, 0], self.mate)
            c.start()
            return e, buf, copies, c

        def finish(self, state):
            e, buf, copies, c0 = state
            g_s, g_r, f_s, f_r = self.gather_sems
            forwards = [c0]
            for i in range(1, self.count):
                copies[i - 1].wait_recv()
                got = buf.at[self.rows((self.high + self.count - i) % self.count, self.low), :]
                f = remote(got, got, f_s.at[e, i], f_r.at[e, i], self.mate)
                f.start()
                forwards.append(f)
            for c in copies:
                c.wait_send()
            wait_all(forwards)

    def half(n, h):
        return pl.ds(h * (n // PARTS), n // PARTS)

    rowx = Axis(rows_n, row, on_row, chunk, (rs1, rr1, rs2, rr2),
                (rs1_s, rs1_r, rs2_s, rs2_r), (rg_s, rg_r, rf_s, rf_r))
    colx = Axis(cols_n, col, on_col, block, (cs1, cr1, cs2, cr2),
                (cs1_s, cs1_r, cs2_s, cs2_r), (cg_s, cg_r, cf_s, cf_r))

    my_rows = pl.ds(pl.multiple_of(col * block, block), block)
    tok_all[my_rows, :] = tokens[...]
    tok_state = colx.gather(0, tok_all)

    weights = (w_in, w_out)

    def times_left(k, vec):
        pieces_l[...] = pieces(vec)
        t = tile_of(width)

        def step(i, _):
            cs = pl.ds(pl.multiple_of(i * t, t), t)
            out = jnp.dot(pieces_l[...], weights[k][:, cs], preferred_element_type=F32)
            left[k, :, cs] = jnp.sum(out, axis=0, keepdims=True)
            return 0

        lax.fori_loop(0, width // t, step, 0)

    def times_right(k, vec):
        pieces_r[...] = pieces(vec)
        t = 256

        def step(i, _):
            rs = pl.ds(pl.multiple_of(i * t, t), t)
            out = lax.dot_general(
                pieces_r[...], weights[k][rs, :], (((1,), (1,)), ((), ())),
                preferred_element_type=F32,
            )
            right[k, :, rs] = jnp.sum(out, axis=0, keepdims=True)
            return 0

        lax.fori_loop(0, depth // t, step, 0)

    def matmul_nn(a, w, h):
        n = width // PARTS
        t = tile_of(n)

        def step(i, _):
            cs = pl.ds(pl.multiple_of(h * n + i * t, LANES), t)
            part[:, cs] = jnp.dot(a[...], w[:, cs], preferred_element_type=F32)
            return 0

        lax.fori_loop(0, n // t, step, 0)

    def matmul_nt(a, w, h):
        n = depth // PARTS
        t = tile_of(n)

        def step(i, _):
            cs = pl.ds(pl.multiple_of(h * n + i * t, LANES), t)
            outp[:, cs] = lax.dot_general(
                a[...], w[cs, :], (((1,), (1,)), ((), ())), preferred_element_type=F32
            )
            return 0

        lax.fori_loop(0, n // t, step, 0)

    def square_sum(vec):
        return jnp.sum(vec * vec, axis=1, keepdims=True)

    def send_left(it, k, squares):
        p_buf[it, k, row, :, :width] = left[k]
        p_buf[it, k, row, :, width:] = jnp.broadcast_to(squares, (1, LANES))
        return row_send(p_buf.at[it, k], p_s.at[it, k], p_r.at[it, k])

    def send_right(it, k, squares):
        q_buf[it, k, col, :, :depth] = right[k]
        q_buf[it, k, col, :, depth:] = jnp.broadcast_to(squares, (1, LANES))
        return col_send(q_buf.at[it, k], q_s.at[it, k], q_r.at[it, k])

    def right_half(it, k, copies):
        wait_all(copies)
        summed = slot_sum(p_buf.at[it, k], rows_n)
        vec = summed[:, :width]
        if it > 0:
            vec = vec / jnp.sqrt(summed[:, width : width + 1] + EPSILON)
        left[k] = vec
        times_right(k, vec)
        return send_right(it, k, square_sum(left[k]))

    def left_half(k, copies):
        wait_all(copies)
        summed = slot_sum(q_buf.at[0, k], cols_n)
        vec = summed[:, :depth] / jnp.sqrt(summed[:, depth : depth + 1] + EPSILON)
        times_left(k, vec)
        return send_left(1, k, square_sum(vec))

    def last_half(k, copies):
        wait_all(copies)
        summed = slot_sum(q_buf.at[1, k], cols_n)
        norm = jnp.sqrt(summed[:, depth : depth + 1] + EPSILON)
        v_units[k : k + 1, :] = left[k] / norm
        right[k] = summed[:, :depth] / norm
        n_buf[k, row] = jnp.broadcast_to(square_sum(right[k]), (1, LANES))
        return row_send(n_buf.at[k], n_s.at[k], n_r.at[k])

    def sigma_of(k, copies):
        wait_all(copies)
        sigma = jnp.sqrt(slot_sum(n_buf.at[k], rows_n)[:, 0:1] + EPSILON)
        u_next[k : k + 1, :] = right[k] / sigma
        return sigma, gains[k] / sigma

    zero = jnp.zeros((1, 1), F32)
    loads[0].wait()
    times_left(0, u_start[0:1, :])
    p0 = send_left(0, 0, zero)
    loads[1].wait()
    times_left(1, u_start[1:2, :])
    p1 = send_left(0, 1, zero)
    q0 = right_half(0, 0, p0)
    colx.finish(tok_state)
    matmul_nn(tok_all, w_in, 0)
    f0 = rowx.first(0, 0, part)
    q1 = right_half(0, 1, p1)
    p0 = left_half(0, q0)
    matmul_nn(tok_all, w_in, 1)
    f1 = rowx.first(0, 1, part)
    s0 = rowx.second(0, 0, part, hid, f0)
    p1 = left_half(1, q1)
    q0 = right_half(1, 0, p0)
    s1 = rowx.second(0, 1, part, hid, f1)
    q1 = right_half(1, 1, p1)
    n0 = last_half(0, q0)
    rowx.last(0, 0, hid, s0)
    rowx.last(0, 1, hid, s1)
    sigma_in, scale_in = sigma_of(0, n0)

    base = row * chunk

    def act_step(i, _):
        rs = pl.ds(pl.multiple_of(i * 16, 16), 16)
        h = hid[rs, :] * scale_in
        cdf = 0.5 * (1.0 + lax.erf(h * ROOT_HALF))
        slopes[rs, :] = cdf + h * jnp.exp(-0.5 * h * h) * INV_ROOT_TWO_PI
        act_all[pl.ds(pl.multiple_of(base + i * 16, 16), 16), :] = (h * cdf).astype(BF16)
        return 0

    lax.fori_loop(0, chunk // 16, act_step, 0)
    state = rowx.gather(0, act_all)
    n1 = last_half(1, q1)
    rowx.finish(state)

    matmul_nt(act_all, w_out, 0)
    f0 = colx.first(0, 0, outp)
    matmul_nt(act_all, w_out, 1)
    f1 = colx.first(0, 1, outp)
    sigma_out, scale_out = sigma_of(1, n1)
    s0 = colx.second(0, 0, outp, out_own, f0)
    s1 = colx.second(0, 1, outp, out_own, f1)
    colx.last(0, 0, out_own, s0)
    colx.last(0, 1, out_own, s1)
    loss_scale = 1.0 / jnp.sqrt(jnp.float32(total))
    g_all[my_rows, :] = (
        (scale_out * out_own[...] - target[...].astype(F32)) * loss_scale
    ).astype(BF16)
    colx.finish(colx.gather(1, g_all))

    matmul_nn(g_all, w_out, 0)
    f0 = rowx.first(1, 0, part)
    matmul_nn(g_all, w_out, 1)
    f1 = rowx.first(1, 1, part)
    s0 = rowx.second(1, 0, part, own, f0)
    s1 = rowx.second(1, 1, part, own, f1)
    rowx.last(1, 0, own, s0)
    rowx.last(1, 1, own, s1)

    def grad_step(i, sums):
        rs = pl.ds(pl.multiple_of(i * 16, 16), 16)
        ra = pl.ds(pl.multiple_of(base + i * 16, 16), 16)
        d = own[rs, :]
        grad = (scale_out * d * slopes[rs, :]).astype(BF16)
        gh_all[ra, :] = grad
        a = jnp.sum(grad.astype(F32) * hid[rs, :], axis=0, keepdims=True)
        b = jnp.sum(act_all[ra, :].astype(F32) * d, axis=0, keepdims=True)
        return sums[0] + a, sums[1] + b

    zeros = jnp.zeros((1, width), F32)
    sum_in, sum_out = lax.fori_loop(0, chunk // 16, grad_step, (zeros, zeros))
    state = rowx.gather(1, gh_all)
    tr_buf[row, 0:1] = jnp.broadcast_to(jnp.sum(sum_in, axis=1, keepdims=True), (1, LANES))
    tr_buf[row, 1:2] = jnp.broadcast_to(jnp.sum(sum_out, axis=1, keepdims=True), (1, LANES))
    tr_copies = row_send(tr_buf, tr_s, tr_r)
    rowx.finish(state)
    wait_all(tr_copies)
    tc_buf[col] = slot_sum(tr_buf, rows_n)
    tc_copies = col_send(tc_buf, tc_s, tc_r)

    matmul_nt(gh_all, w_in, 0)
    f0 = colx.first(1, 0, outp)
    matmul_nt(gh_all, w_in, 1)
    f1 = colx.first(1, 1, outp)
    s0 = colx.second(1, 0, outp, out_own, f0)
    s1 = colx.second(1, 1, outp, out_own, f1)
    wait_all(tc_copies)
    traces = slot_sum(tc_buf, cols_n)
    coeffs[0:1, :] = jnp.broadcast_to(scale_in, (1, LANES))
    coeffs[1:2, :] = jnp.broadcast_to(scale_out, (1, LANES))
    coeffs[2:3, :] = scale_in * traces[0:1] / sigma_in
    coeffs[3:4, :] = scale_out * traces[1:2] / sigma_out
    colx.last(1, 0, out_own, s0)
    colx.last(1, 1, out_own, s1)
    grad_tokens[...] = (scale_in * out_own[...]).astype(BF16)


def grads_body(tok, gh, g, act, u, v, coeffs, gin, gout):
    width = gh.shape[1]
    t = tile_of(width)
    for k, (a, b, out) in enumerate(((tok, gh, gin), (g, act, gout))):
        turned = jnp.transpose(a[...])
        shift = jnp.broadcast_to(u[k : k + 1, :] * coeffs[2 + k : 3 + k, 0:1], (LANES, u.shape[1]))
        shift = jnp.transpose(shift)[:, 0:1]
        scale = coeffs[k : k + 1, 0:1]
        for i in range(width // t):
            cs = slice(i * t, (i + 1) * t)
            prod = jnp.dot(turned, b[:, cs], preferred_element_type=F32)
            out[:, cs] = (scale * prod - shift * v[k : k + 1, cs]).astype(BF16)


def shards(rows_n, cols_n, tokens, target, w_in, w_out, gains, u_start):
    block, depth = tokens.shape
    width = w_in.shape[1]
    total = block * cols_n
    chunk = total // rows_n
    vmem = pl.BlockSpec(memory_space=pltpu.VMEM)
    dma = pltpu.SemaphoreType.DMA
    S = pltpu.VMEM
    ys, zs = rows_n // 2, cols_n // 2
    row_part = (2, PARTS, ys, chunk, width // PARTS)
    col_part = (2, PARTS, zs, block, depth // PARTS)
    tok_all, act_all, g_all, gh_all, u_next, v_units, coeffs, grad_tokens = pl.pallas_call(
        functools.partial(body, rows_n, cols_n),
        out_shape=(
            jax.ShapeDtypeStruct((total, depth), BF16),
            jax.ShapeDtypeStruct((total, width), BF16),
            jax.ShapeDtypeStruct((total, depth), BF16),
            jax.ShapeDtypeStruct((total, width), BF16),
            jax.ShapeDtypeStruct((2, depth), F32),
            jax.ShapeDtypeStruct((2, width), F32),
            jax.ShapeDtypeStruct((4, LANES), F32),
            jax.ShapeDtypeStruct((block, depth), BF16),
        ),
        in_specs=[vmem, vmem, pl.BlockSpec(memory_space=pltpu.SMEM), vmem]
        + [pl.BlockSpec(memory_space=pl.ANY)] * 2,
        out_specs=[vmem] * 8,
        scratch_shapes=[
            S((depth, width), BF16), S((depth, width), BF16),
            S((total, width), F32),
            S((chunk, width), F32), S((chunk, width), F32), S((chunk, width), F32),
            S(row_part, BF16), S(row_part, BF16), S(row_part, BF16), S(row_part, BF16),
            S((total, depth), F32), S((block, depth), F32),
            S(col_part, BF16), S(col_part, BF16), S(col_part, BF16), S(col_part, BF16),
            S((16, depth), BF16), S((16, width), BF16),
            S((2, 1, width), F32), S((2, 1, depth), F32),
            S((2, 2, rows_n, 1, width + LANES), F32),
            S((2, 2, cols_n, 1, depth + LANES), F32),
            S((2, rows_n, 1, LANES), F32), S((rows_n, 2, LANES), F32), S((cols_n, 2, LANES), F32),
            dma((2,)),
            dma((2, 2, rows_n)), dma((2, 2, rows_n)),
            dma((2, 2, cols_n)), dma((2, 2, cols_n)),
            dma((2, rows_n)), dma((2, rows_n)),
            dma((rows_n,)), dma((rows_n,)),
            dma((cols_n,)), dma((cols_n,)),
        ]
        + [dma((2, PARTS, ys))] * 4
        + [dma((2, PARTS, zs))] * 4
        + [dma((2, ys))] * 4
        + [dma((2, zs))] * 4,
        compiler_params=pltpu.CompilerParams(
            collective_id=0, has_side_effects=True, vmem_limit_bytes=58 * 1024 * 1024
        ),
    )(tokens, target, gains, u_start, w_in, w_out)
    rows = 256
    whole = lambda shape: pl.BlockSpec(shape, lambda i: (0, 0))
    side = lambda n: pl.BlockSpec((n, rows), lambda i: (0, i))
    grad_in, grad_out = pl.pallas_call(
        grads_body,
        grid=(depth // rows,),
        out_shape=(
            jax.ShapeDtypeStruct((depth, width), BF16),
            jax.ShapeDtypeStruct((depth, width), BF16),
        ),
        in_specs=[
            side(total), whole((total, width)), side(total), whole((total, width)),
            side(2), whole((2, width)), whole((4, LANES)),
        ],
        out_specs=[pl.BlockSpec((rows, width), lambda i: (i, 0))] * 2,
        compiler_params=pltpu.CompilerParams(vmem_limit_bytes=40 * 1024 * 1024),
    )(tok_all, gh_all, g_all, act_all, u_next, v_units, coeffs)
    return grad_tokens, grad_in, grad_out, u_next


def solution(mesh):
    placed = (
        P("col", "row"),
        P("col", "row"),
        P("row", "col"),
        P("row", "col"),
        P(),
        P(None, "row"),
    )
    return jax.shard_map(
        functools.partial(shards, mesh.shape["row"], mesh.shape["col"]),
        mesh=mesh,
        in_specs=placed,
        out_specs=(P("col", "row"), P("row", "col"), P("row", "col"), P(None, "row")),
        check_vma=False,
    )
```

time: 190 us -> 155 us (0.82)
  the two profiles are of different devices: /device:TPU:26 before, /device:TPU:0 now
where the time goes in v2:
time: 155 us; the launch traced here: 154 us
  Pallas kernels  144 us (93%)
  local copies, waits for them, and re-layouts  9.34 us (6%)
    pallas_call x1, Pallas kernels, shards(): pl.pallas_call(functools.partial(body, rows_n, cols_n), out_shape=(jax.Sh...  135 us
    unnamed x16, local copies, waits for them, and re-layouts  9.34 us
    pallas_call x1, Pallas kernels, shards(): pl.pallas_call(grads_body, grid=(depth // rows,), out_shape=(jax.ShapeDty...  8.98 us

profile of v2, /device:TPU:0, one launch (start us, length us, event | category | flops | bytes accessed | tf_op | source)
XLA Modules:
  0.0 154.3 jit_solution(13238733859067940738)
XLA Ops:
  0.6 135.3 %shard_map.93 = (bf16[256,1536]{1,0:T(8,128)(2,1)}, bf16[256,3072]{1,0:T(8,128)(2,1)}, bf16[256,1536]{1,0:T(8,128)(2,1)}, bf16[256,3072]{1,0:T(8,128)(2,1)}, f32...) custom-call(bf16[32,1536]{1,0:T(8,128)(2,1)} %tokens.1, ...), custom_call_target="tpu_custom_call" | custom-call | tf_op jit(solution)/shard_map/pallas_call | solution.py:427
  135.9 0.0 copy-start
  135.9 1.4 copy-done
  137.3 0.0 copy-start.1
  137.3 1.4 copy-done.1
  138.7 0.0 copy-start.2
  138.7 1.1 copy-done.2
  139.9 0.0 copy-start.3
  139.9 1.1 copy-done.3
  141.0 0.0 copy-start.4
  141.0 0.7 copy-done.4
  141.7 0.0 copy-start.5
  141.7 0.7 copy-done.5
  142.4 0.0 copy-start.6
  142.5 0.7 copy-done.6
  143.1 9.0 %shard_map.94 = (bf16[1536,3072]{1,0:T(8,128)(2,1)}, bf16[1536,3072]{1,0:T(8,128)(2,1)}) custom-call(bf16[256,1536]{1,0:T(8,128)(2,1)S(1)} %copy-done.2, bf16[256,3072]{1,0:T(8,128)(2,1)S(1)} %copy-done.1, bf16[256,1536]{1,0:T(8,128)(2,1)S(1)} %copy-done.3, bf16[256,3072]{1,0:T(8,128)(2,1)S(1)} %copy-done, f32[2,1536]{1,0:T(2,128)S(1)} %copy-done.4, ...), custom_call_target="tpu_custom_call" | custom-call | tf_op jit(solution)/shard_map/pallas_call | solution.py:472
  152.1 1.5 copy.12
  153.7 0.6 copy.13
Async XLA Ops:
  135.9 1.4 copy-start
  137.3 1.4 copy-start.1
  138.7 1.1 copy-start.2
  139.9 1.1 copy-start.3
  141.0 0.7 copy-start.4
  141.7 0.7 copy-start.5
  142.4 0.7 copy-start.6

commit v3 on v2

--- a/solution.py
+++ b/solution.py
@@ -160,32 +160,49 @@
                 acc = acc + r2[e, h, i - 1].astype(F32)
             dst[:, cols] = acc
 
-        def gather(self, e, buf):
+        def piece(self, high, h):
+            n = self.size // PARTS
+            start = (high * 2 + self.low) * self.size + h * n
+            return pl.ds(pl.multiple_of(start, n), n)
+
+        def gather(self, e, h, buf):
             g_s, g_r, f_s, f_r = self.gather_sems
-            mine = buf.at[self.rows(self.high, self.low), :]
+            mine = buf.at[self.piece(self.high, h), :]
             copies = []
             for i in range(1, self.count):
-                c = remote(mine, mine, g_s.at[e, i], g_r.at[e, i],
+                c = remote(mine, mine, g_s.at[e, h, i], g_r.at[e, h, i],
                            self.dev(((self.high + i) % self.count) * 2 + self.low))
                 c.start()
                 copies.append(c)
-            c = remote(mine, mine, f_s.at[e, 0], f_r.at[e, 0], self.mate)
+            c = remote(mine, mine, f_s.at[e, h, 0], f_r.at[e, h, 0], self.mate)
             c.start()
-            return e, buf, copies, c
-
-        def finish(self, state):
-            e, buf, copies, c0 = state
+            return e, h, buf, copies, c
+
+        def forward(self, states):
             g_s, g_r, f_s, f_r = self.gather_sems
-            forwards = [c0]
-            for i in range(1, self.count):
-                copies[i - 1].wait_recv()
-                got = buf.at[self.rows((self.high + self.count - i) % self.count, self.low), :]
-                f = remote(got, got, f_s.at[e, i], f_r.at[e, i], self.mate)
-                f.start()
-                forwards.append(f)
-            for c in copies:
-                c.wait_send()
+            forwards = []
+            for e, h, buf, copies, c0 in states:
+                forwards.append(c0)
+                for i in range(1, self.count):
+                    copies[i - 1].wait_recv()
+                    got = buf.at[self.piece((self.high + self.count - i) % self.count, h), :]
+                    f = remote(got, got, f_s.at[e, h, i], f_r.at[e, h, i], self.mate)
+                    f.start()
+                    forwards.append(f)
+            return states, forwards
+
+        def complete(self, moves):
+            states, forwards = moves
+            for _, _, _, copies, _ in states:
+                for c in copies:
+                    c.wait_send()
             wait_all(forwards)
+
+        def finish(self, states):
+            self.complete(self.forward(states))
+
+        def gather_all(self, e, buf):
+            return [self.gather(e, h, buf) for h in range(PARTS)]
 
     def half(n, h):
         return pl.ds(h * (n // PARTS), n // PARTS)
@@ -197,7 +214,7 @@
 
     my_rows = pl.ds(pl.multiple_of(col * block, block), block)
     tok_all[my_rows, :] = tokens[...]
-    tok_state = colx.gather(0, tok_all)
+    tok_state = colx.gather_all(0, tok_all)
 
     weights = (w_in, w_out)
 
@@ -304,8 +321,9 @@
     loads[1].wait()
     times_left(1, u_start[1:2, :])
     p1 = send_left(0, 1, zero)
+    tok_moves = colx.forward(tok_state)
     q0 = right_half(0, 0, p0)
-    colx.finish(tok_state)
+    colx.complete(tok_moves)
     matmul_nn(tok_all, w_in, 0)
     f0 = rowx.first(0, 0, part)
     q1 = right_half(0, 1, p1)
@@ -332,8 +350,11 @@
         act_all[pl.ds(pl.multiple_of(base + i * 16, 16), 16), :] = (h * cdf).astype(BF16)
         return 0
 
-    lax.fori_loop(0, chunk // 16, act_step, 0)
-    state = rowx.gather(0, act_all)
+    steps = chunk // 16 // PARTS
+    state = []
+    for h in range(PARTS):
+        lax.fori_loop(h * steps, (h + 1) * steps, act_step, 0)
+        state.append(rowx.gather(0, h, act_all))
     n1 = last_half(1, q1)
     rowx.finish(state)
 
@@ -350,7 +371,7 @@
     g_all[my_rows, :] = (
         (scale_out * out_own[...] - target[...].astype(F32)) * loss_scale
     ).astype(BF16)
-    colx.finish(colx.gather(1, g_all))
+    colx.finish(colx.gather_all(1, g_all))
 
     matmul_nn(g_all, w_out, 0)
     f0 = rowx.first(1, 0, part)
@@ -372,8 +393,12 @@
         return sums[0] + a, sums[1] + b
 
     zeros = jnp.zeros((1, width), F32)
-    sum_in, sum_out = lax.fori_loop(0, chunk // 16, grad_step, (zeros, zeros))
-    state = rowx.gather(1, gh_all)
+    sums = (zeros, zeros)
+    state = []
+    for h in range(PARTS):
+        sums = lax.fori_loop(h * steps, (h + 1) * steps, grad_step, sums)
+        state.append(rowx.gather(1, h, gh_all))
+    sum_in, sum_out = sums
     tr_buf[row, 0:1] = jnp.broadcast_to(jnp.sum(sum_in, axis=1, keepdims=True), (1, LANES))
     tr_buf[row, 1:2] = jnp.broadcast_to(jnp.sum(sum_out, axis=1, keepdims=True), (1, LANES))
     tr_copies = row_send(tr_buf, tr_s, tr_r)
@@ -460,8 +485,8 @@
         ]
         + [dma((2, PARTS, ys))] * 4
         + [dma((2, PARTS, zs))] * 4
-        + [dma((2, ys))] * 4
-        + [dma((2, zs))] * 4,
+        + [dma((2, PARTS, ys))] * 4
+        + [dma((2, PARTS, zs))] * 4,
         compiler_params=pltpu.CompilerParams(
             collective_id=0, has_side_effects=True, vmem_limit_bytes=58 * 1024 * 1024
         ),
@@ -481,7 +506,7 @@
             side(2), whole((2, width)), whole((4, LANES)),
         ],
         out_specs=[pl.BlockSpec((rows, width), lambda i: (i, 0))] * 2,
-        compiler_params=pltpu.CompilerParams(vmem_limit_bytes=40 * 1024 * 1024),
+        compiler_params=pltpu.CompilerParams(vmem_limit_bytes=60 * 1024 * 1024),
     )(tok_all, gh_all, g_all, act_all, u_next, v_units, coeffs)
     return grad_tokens, grad_in, grad_out, u_next
 

time: 155 us -> 145 us (0.935)
  local copies, waits for them, and re-layouts: 9.34 us -> 2.84 us
  Pallas kernels: 144 us -> 141 us
    unnamed x16 -> x2, local copies, waits for them, and re-layouts: 9.34 us -> 2.84 us
    pallas_call x1, Pallas kernels: 135 us -> 130 us  [shards(): pl.pallas_call(functools.partial(body, rows_n, cols_n), out_shape=(jax.Sh...]
    pallas_call x1, Pallas kernels: 8.98 us -> 11 us  [shards(): pl.pallas_call(grads_body, grid=(depth // rows,), out_shape=(jax.ShapeDty...]
where the time goes in v3:
time: 145 us
  Pallas kernels  141 us (97%)
  local copies, waits for them, and re-layouts  2.84 us (2%)
    pallas_call x1, Pallas kernels, shards(): pl.pallas_call(functools.partial(body, rows_n, cols_n), out_shape=(jax.Sh...  130 us
    pallas_call x1, Pallas kernels, shards(): pl.pallas_call(grads_body, grid=(depth // rows,), out_shape=(jax.ShapeDty...  11 us

profile of v3, /device:TPU:0, one launch (start us, length us, event | category | flops | bytes accessed | tf_op | source)
XLA Modules:
  0.0 144.5 jit_solution(2268679029682081242)
XLA Ops:
  0.6 130.1 %shard_map.93 = (bf16[256,1536]{1,0:T(8,128)(2,1)}, bf16[256,3072]{1,0:T(8,128)(2,1)}, bf16[256,1536]{1,0:T(8,128)(2,1)}, bf16[256,3072]{1,0:T(8,128)(2,1)}, f32...) custom-call(bf16[32,1536]{1,0:T(8,128)(2,1)} %tokens.1, ...), custom_call_target="tpu_custom_call" | custom-call | tf_op jit(solution)/shard_map/pallas_call | solution.py:452
  130.7 11.0 %shard_map.94 = (bf16[1536,3072]{1,0:T(8,128)(2,1)}, bf16[1536,3072]{1,0:T(8,128)(2,1)}) custom-call(bf16[256,1536]{1,0:T(8,128)(2,1)} %get-tuple-element.15.tok, bf16[256,3072]{1,0:T(8,128)(2,1)} %get-tuple-element.16.gh, bf16[256,1536]{1,0:T(8,128)(2,1)} %get-tuple-element.17.g, bf16[256,3072]{1,0:T(8,128)(2,1)} %get-tuple-element.18.act, ...), custom_call_target="tpu_custom_call" | custom-call | tf_op jit(solution)/shard_map/pallas_call | solution.py:497
  141.7 1.5 %copy.12 = bf16[32,1536]{1,0:T(8,128)(2,1)} copy(bf16[32,1536]{1,0:T(8,128)(2,1)} %get-tuple-element.28) | data formatting | bytes 196608
  143.2 1.3 copy.13

commit v4 on v3

--- a/solution.py
+++ b/solution.py
@@ -220,7 +220,7 @@
 
     def times_left(k, vec):
         pieces_l[...] = pieces(vec)
-        t = tile_of(width)
+        t = 768 if width % 768 == 0 else LANES
 
         def step(i, _):
             cs = pl.ds(pl.multiple_of(i * t, t), t)
@@ -232,7 +232,7 @@
 
     def times_right(k, vec):
         pieces_r[...] = pieces(vec)
-        t = 256
+        t = 768 if depth % 768 == 0 else LANES
 
         def step(i, _):
             rs = pl.ds(pl.multiple_of(i * t, t), t)

time: 145 us -> 144 us (level)
  no operation moved by 1% of the time
where the time goes in v4:
time: 144 us; the launch traced here: 143 us
  Pallas kernels  140 us (97%)
  local copies, waits for them, and re-layouts  2.84 us (2%)
    pallas_call x1, Pallas kernels, shards(): pl.pallas_call(functools.partial(body, rows_n, cols_n), out_shape=(jax.Sh...  129 us
    pallas_call x1, Pallas kernels, shards(): pl.pallas_call(grads_body, grid=(depth // rows,), out_shape=(jax.ShapeDty...  11 us

profile of v4, /device:TPU:0, one launch (start us, length us, event | category | flops | bytes accessed | tf_op | source)
XLA Modules:
  0.0 143.2 jit_solution(2441532499271533029)
XLA Ops:
  0.6 128.8 %shard_map.93 = (bf16[256,1536]{1,0:T(8,128)(2,1)}, bf16[256,3072]{1,0:T(8,128)(2,1)}, bf16[256,1536]{1,0:T(8,128)(2,1)}, bf16[256,3072]{1,0:T(8,128)(2,1)}, f32...) custom-call(bf16[32,1536]{1,0:T(8,128)(2,1)} %tokens.1, ...), custom_call_target="tpu_custom_call" | custom-call | tf_op jit(solution)/shard_map/pallas_call | solution.py:452
  129.4 11.0 %shard_map.94 = (bf16[1536,3072]{1,0:T(8,128)(2,1)}, bf16[1536,3072]{1,0:T(8,128)(2,1)}) custom-call(bf16[256,1536]{1,0:T(8,128)(2,1)} %get-tuple-element.15.tok, bf16[256,3072]{1,0:T(8,128)(2,1)} %get-tuple-element.16.gh, bf16[256,1536]{1,0:T(8,128)(2,1)} %get-tuple-element.17.g, bf16[256,3072]{1,0:T(8,128)(2,1)} %get-tuple-element.18.act, ...), custom_call_target="tpu_custom_call" | custom-call | tf_op jit(solution)/shard_map/pallas_call | solution.py:497
  140.4 1.5 %copy.12 = bf16[32,1536]{1,0:T(8,128)(2,1)} copy(bf16[32,1536]{1,0:T(8,128)(2,1)} %get-tuple-element.28) | data formatting | bytes 196608
  141.9 1.3 copy.13
